TPU v7x, 32 devices: a whole 2x2x4 slice. The times are simulated.
32 devices in a mesh: row: 4 (over z), col: 8 (over y, x, core).
Axes of the slice: x: 2, y: 2, z: 4, core: 2. Of those that a mesh axis runs over, the one named last changes fastest.
Arguments:
- tokens: bfloat16 [16384, 1024], P('row', 'col'), may hold values from -6 to 6
- cotangent: bfloat16 [16384, 1024], P('row', 'col'), may hold values from -6 to 6
- adapter_ids: int32 [16, 4], P('row'), may hold values from 0 to 7
- qkv_weight: bfloat16 [2, 1024, 3, 1024], P(None, 'row', None, 'col'), may hold values from -0.09375 to 0.09375
- qkv_bias: bfloat16 [2, 3, 1024], P(None, None, 'col'), may hold values from -1.796875 to 1.796875
- proj_weight: bfloat16 [2, 1024, 1024], P(None, 'col', 'row'), may hold values from -4 to 4
- proj_bias: bfloat16 [2, 1024], P(None, 'col'), may hold values from -1.796875 to 1.796875
- up_weight: bfloat16 [2, 1024, 4096], P(None, 'row', 'col'), may hold values from -0.09375 to 0.09375
- up_bias: bfloat16 [2, 4096], P(None, 'col'), may hold values from -1.796875 to 1.796875
- down_weight: bfloat16 [2, 4096, 1024], P(None, 'col', 'row'), may hold values from -0.09375 to 0.09375
- down_bias: bfloat16 [2, 1024], P(None, 'col'), may hold values from -1.796875 to 1.796875
- first_gain: bfloat16 [2, 1024], P(None, 'col'), may hold values from 0.5 to 1.5
- first_shift: bfloat16 [2, 1024], P(None, 'col'), may hold values from -1.796875 to 1.796875
- second_gain: bfloat16 [2, 1024], P(None, 'col'), may hold values from 0.5 to 1.5
- second_shift: bfloat16 [2, 1024], P(None, 'col'), may hold values from -1.796875 to 1.796875
- qkv_lower: bfloat16 [2, 8, 1024, 16], replicated, may hold values from -0.1875 to 0.1875
- qkv_raise: bfloat16 [2, 8, 16, 3, 1024], replicated, may hold values from -0.75 to 0.75
- proj_lower: bfloat16 [2, 8, 1024, 16], replicated, may hold values from -4 to 4
- proj_raise: bfloat16 [2, 8, 16, 1024], replicated, may hold values from -0.75 to 0.75
- up_lower: bfloat16 [2, 8, 1024, 16], replicated, may hold values from -0.1875 to 0.1875
- up_raise: bfloat16 [2, 8, 16, 4096], replicated, may hold values from -0.75 to 0.75
- down_lower: bfloat16 [2, 8, 4096, 16], replicated, may hold values from -0.09375 to 0.09375
- down_raise: bfloat16 [2, 8, 16, 1024], replicated, may hold values from -0.75 to 0.75
Outputs:
- result: float32 [16384, 1024], P('row', 'col')
- input_grad: float32 [16384, 1024], P('row', 'col')
- grad_qkv_lower: float32 [2, 8, 1024, 16], P(None, None, 'col')
- grad_qkv_raise: float32 [2, 8, 16, 3, 1024], P(None, None, None, None, 'col')
- grad_proj_lower: float32 [2, 8, 1024, 16], P(None, None, 'col')
- grad_proj_raise: float32 [2, 8, 16, 1024], P(None, None, None, 'col')
- grad_up_lower: float32 [2, 8, 1024, 16], P(None, None, 'col')
- grad_up_raise: float32 [2, 8, 16, 4096], P(None, None, None, 'col')
- grad_down_lower: float32 [2, 8, 4096, 16], P(None, None, 'col')
- grad_down_raise: float32 [2, 8, 16, 1024], P(None, None, None, 'col')
Inputs may be any that keep to these rules, and one draw needn't show every extreme that they name: adapter_ids[s, k] names the adapter of sequence s at site k.
All inputs are finite; a program needn't handle non-finite values.
Results may differ from a plain program's by a relative error of at most 0.018.
Values may be sent and summed in bfloat16 or wider, within the bound.
A program may use at most 256 MiB of HBM per device.

v0:
```python
import functools
import math

import jax
import jax.numpy as jnp
from jax import lax
from jax.experimental import pallas as pl
from jax.experimental.pallas import tpu as pltpu
from jax.sharding import PartitionSpec as P

HD = 64
LEN = 1024
BLOCK = 256
BLOCKS = LEN // BLOCK
EPSILON = 1e-05
SCALE = HD**-0.5
ROOT = (2.0 / 3.141592653589793) ** 0.5
MESH = pl.DeviceIdType.MESH
F32 = jnp.float32
BF16 = jnp.bfloat16


ROW_FIRST = (("z", 0, 1), ("z", 1, 0))
ROW_SECOND = ((0, "z", 1), (1, "z", 0))
ORDERS = (
    {"qkv": (ROW_FIRST,), "proj": (ROW_SECOND,), "up": (ROW_FIRST,) * 2, "down": (ROW_SECOND, ROW_FIRST)},
    {"qkv": (ROW_SECOND,), "proj": (ROW_FIRST,), "up": (ROW_SECOND,) * 2, "down": (ROW_SECOND,) * 2},
)
CUTS = {kind: 2 * len(pairs) for kind, pairs in ORDERS[0].items()}
KINDS = ("qkv", "proj", "up", "down")
DEPTH = 4
FUSED = True
LINK = 90e3
DELAY, ROW_DELAY = 2.0, 4.0
FIRST = 12.0


def transfer_plan(order, n_row):
    masks, rows, steps = [0], False, []
    for d in order:
        if d == "z":
            steps += [(("z", hop), tuple(masks), rows) for hop in range(1, n_row)]
            rows = True
        else:
            steps.append((d, tuple(masks), rows))
            masks = masks + [m ^ d for m in masks]
    steps.append((None, tuple(masks), rows))
    return steps


def transfer_schedule(pieces, n_row, tasks):
    cost, parts = {}, {}
    for k, (name, order, size) in enumerate(pieces):
        parts.setdefault(name, set()).add(k)
        for p, (d, masks, rows) in enumerate(transfer_plan(order, n_row)[:-1]):
            axis = "z" if isinstance(d, tuple) else d
            cost[k, p] = (axis, 2 * len(masks) * (n_row if rows else 1) * size / LINK)
    ready = {d: [] for d, _ in cost.values()}
    free = {d: 0.0 if d == "z" else FIRST for d in ready}
    flight = {d: [] for d in ready}
    for k in range(len(pieces)):
        ready[cost[k, 0][0]].append((k, 0))
    tasks, left = list(tasks), {}
    for task in tasks:
        left[task[4]] = left.get(task[4], 0) + 1
    landed, staged, now, ops = {}, {}, 0.0, []

    def stage(name):
        kind, l = name
        if name in landed and name not in staged and landed[name] <= now and not left.get((kind, l - 1)):
            staged[name] = now + 3.0
            ops.append(("stage", kind, l))

    while tasks or any(ready.values()) or any(flight.values()):
        for d in ready:
            while ready[d] and len(flight[d]) < DEPTH:
                k, p = ready[d].pop(0)
                free[d] = max(now, free[d]) + cost[k, p][1]
                flight[d].append((free[d] + (ROW_DELAY if d == "z" else DELAY), k, p))
                ops.append(("start", k, p))
        if tasks:
            for name in list(landed):
                stage(name)
        events = [f for line in flight.values() for f in line]
        event = min(events) if events else None
        due = None
        if tasks:
            need = tasks[0][4]
            due = now if need is None else staged.get(need)
            if due is None and need in landed and not left.get((need[0], need[1] - 1)):
                due = landed[need]
        if due is not None and (event is None or max(due, now) < event[0]):
            now = max(due, now)
            need = tasks[0][4]
            if need is not None and need not in staged:
                continue
            name, l, part, micros, _ = tasks.pop(0)
            left[need] -= 1
            now += micros
            ops.append(("task", name, (l, part)))
            continue
        now, k, p = max(now, event[0]), event[1], event[2]
        d = cost[k, p][0]
        flight[d].remove(event)
        ops.append(("wait", k, p))
        if (k, p + 1) in cost:
            later = ready[cost[k, p + 1][0]]
            later.append((k, p + 1))
            later.sort()
        else:
            name = pieces[k][0]
            parts[name].discard(k)
            if not parts[name]:
                landed[name] = now + 4.0
    return ops


def place_of(group, g, b):
    if group == 2:
        return g + b * (BLOCKS - 1 - 2 * g)
    return g * (BLOCKS // group) + b


def positions(group):
    per = BLOCKS // group
    return tuple(tuple(place_of(group, g, b) for b in range(per)) for g in range(group))


NARROW = 8
CROSS = ((0,), (0,))
TURNED = ((1,), (1,))


def dot(a, b, dims=((1,), (0,))):
    return lax.dot_general(a, b, (dims, ((), ())), preferred_element_type=F32)


def columns(i, size=128):
    if isinstance(i, int):
        return pl.ds(i * size, size)
    return pl.ds(pl.multiple_of(i * size, size), size)


def norm_parts(x):
    center = x - jnp.mean(x, axis=1, keepdims=True)
    inverse = lax.rsqrt(jnp.mean(center * center, axis=1, keepdims=True) + EPSILON)
    return center * inverse, inverse


def norm_grad(grad, scaled, inverse, gain):
    w = grad * gain
    first = jnp.mean(w, axis=1, keepdims=True)
    second = jnp.mean(w * scaled, axis=1, keepdims=True)
    return inverse * (w - first - scaled * second)


def norm_low(x, gain, shift):
    return (norm_parts(x)[0] * gain + shift).astype(BF16)


def pair_state(held):
    group, per = len(held), len(held[0])
    state = {}
    for s in range(per):
        for j in range(group):
            for b in range(per):
                seen = {held[(g - j) % group][b] <= held[g][s] for g in range(group)}
                state[s, j, b] = 0 if len(seen) == 2 else (1 if True in seen else -1)
    return state


def pair_bias(held, g):
    group = len(held)
    bias = {}
    for (s, j, b), state in pair_state(held).items():
        if state == 0:
            keys = place_of(group, lax.rem(g - j + group, group), b)
            bias[s, j, b] = jnp.where(keys <= place_of(group, g, s), 0.0, -1e9).astype(F32)
    return bias


def head_mask(h):
    lane = lax.broadcasted_iota(jnp.int32, (1, 128), 1)
    return (lane // HD) == h


def turning_pair(held, g):
    if len(held) != 2:
        return None, [0.0] * len(held[0])
    at = 1 - g
    return at, [jnp.where(at == n, 1.0, 0.0).astype(F32) for n in range(len(held[0]))]


def both_heads(x):
    return jnp.concatenate([jnp.where(head_mask(h), x, 0).astype(BF16) for h in range(2)], axis=0)


def slots_of(held, j, b, fixed):
    state = pair_state(held)
    return [s for s in range(len(held[0])) if state[s, j, b] > 0 or (state[s, j, b] == 0 and not fixed)]


def attend_strip(held, bias, g, i, q, kvs, out, lse):
    group, per = len(held), len(held[0])
    at, here = turning_pair(held, g)
    wide = 2 * BLOCK
    blocks = [(j, b, slots_of(held, j, b, at is not None)) for j in range(group) for b in range(per)]
    queries = [both_heads(q[i, s * BLOCK : (s + 1) * BLOCK, :] * SCALE) for s in range(per)]
    scores = {s: [] for s in range(per)}
    for j, b, slots in blocks:
        if slots:
            keys = kvs[j][i, b * BLOCK : (b + 1) * BLOCK, :128]
            score = dot(keys, jnp.concatenate([queries[s] for s in slots], axis=0), TURNED)
            for n, s in enumerate(slots):
                part = score[:, n * wide : (n + 1) * wide]
                scores[s].append(((j, b), part + bias[s, j, b] if (s, j, b) in bias and at is None else part))
    turned = {(j, b): kvs[j][i, b * BLOCK : (b + 1) * BLOCK, 128:].T for j, b, slots in blocks if slots}

    def weigh(e, values):
        e = e.astype(BF16)
        return jnp.concatenate(
            [dot(values[h * HD : (h + 1) * HD], e[:, h * BLOCK : (h + 1) * BLOCK]) for h in range(2)], axis=1
        )

    extra = None
    if at is not None:
        moving = pl.ds(pl.multiple_of(at * BLOCK, BLOCK), BLOCK)
        score = dot(kvs[1][i, moving, :128], both_heads(q[i, moving, :] * SCALE), TURNED)
        top = jnp.max(score, axis=0, keepdims=True)
        e = jnp.exp(score - top)
        extra = (top, jnp.sum(e, axis=0, keepdims=True), weigh(e, kvs[1][i, moving, 128:].T))
    for s in range(per):
        tops = [jnp.max(x, axis=0, keepdims=True) for _, x in scores[s]]
        if extra:
            tops.append(extra[0] + (here[s] - 1.0) * 1e9)
        top = functools.reduce(jnp.maximum, tops)
        total, made = 0.0, 0.0
        for place, score in scores[s]:
            e = jnp.exp(score - top)
            total = total + jnp.sum(e, axis=0, keepdims=True)
            made = made + weigh(e, turned[place])
        if extra:
            weight = jnp.exp(tops[-1] - top) * here[s]
            total = total + weight * extra[1]
            made = made + weight * extra[2]
        made = made / total
        level = top + jnp.log(total)
        rows = pl.ds(s * BLOCK, BLOCK)
        for h in range(2):
            lse[i, h : h + 1, rows] = level[:, h * BLOCK : (h + 1) * BLOCK]
        both = jnp.concatenate([made[:, :BLOCK], made[:, BLOCK:]], axis=0)
        out[rows, columns(i)] = both.T.astype(BF16)


def attend_back_strip(held, bias, g, i, q, lse, out, grad, kvs, gq, gkvs):
    group, per = len(held), len(held[0])
    at, here = turning_pair(held, g)

    def slot(rows):
        up = grad[rows, columns(i)]
        product = (up.astype(F32) * out[rows, columns(i)].astype(F32)).T
        inner = [jnp.sum(product[h * HD : (h + 1) * HD], axis=0, keepdims=True) for h in range(2)]
        level = [lse[i, h : h + 1, rows] for h in range(2)]
        return [
            both_heads(q[i, rows, :] * SCALE), both_heads(up),
            jnp.concatenate(inner, axis=1), jnp.concatenate(level, axis=1),
        ]

    def block(parts, keys, values):
        query, given = [jnp.concatenate([part[n] for part in parts], axis=0) for n in (0, 1)]
        inner, level = [jnp.concatenate([part[n] for part in parts], axis=1) for n in (2, 3)]
        probs = jnp.exp(dot(keys, query, TURNED) - level)
        g_scores = (probs * (dot(values, given, TURNED) - inner)).astype(BF16)
        turned = keys.T
        made = []
        for n in range(len(parts)):
            pieces = []
            for h in range(2):
                first = (2 * n + h) * BLOCK
                pieces.append(dot(turned[h * HD : (h + 1) * HD], g_scores[:, first : first + BLOCK]))
            made.append(jnp.concatenate(pieces, axis=0))
        return made, dot(g_scores, query), dot(probs.astype(BF16), given)

    slots = [slot(pl.ds(s * BLOCK, BLOCK)) for s in range(per)]
    total = [0.0] * per
    moved = None
    if at is not None:
        moving = pl.ds(pl.multiple_of(at * BLOCK, BLOCK), BLOCK)
        moved = block([slot(moving)], kvs[1][i, moving, :128], kvs[1][i, moving, 128:])
        total = [here[s] * moved[0][0] for s in range(per)]
    for j in range(group):
        for b in range(per):
            rows = pl.ds(b * BLOCK, BLOCK)
            k, v = 0.0, 0.0
            wanted = slots_of(held, j, b, at is not None)
            if wanted:
                parts = []
                for s in wanted:
                    part = list(slots[s])
                    if at is None and (s, j, b) in bias:
                        part[3] = part[3] - bias[s, j, b]
                    parts.append(part)
                made, k, v = block(parts, kvs[j][i, rows, :128], kvs[j][i, rows, 128:])
                for n, s in enumerate(wanted):
                    total[s] = total[s] + made[n]
            if at is not None and j == 1:
                k, v = k + here[b] * moved[1], v + here[b] * moved[2]
            gkvs[j][i, rows, :128] = k.astype(BF16)
            gkvs[j][i, rows, 128:] = v.astype(BF16)
    for s in range(per):
        gq[i, pl.ds(s * BLOCK, BLOCK), :] = (total[s] * SCALE).T.astype(BF16)


def by_rows(count, body, size=128):
    each(count // size, lambda n: body(pl.ds(pl.multiple_of(n * size, size), size)))


def keep(value, red, red_out):
    red[...] = value.astype(BF16)
    red_out[...] = value.T.astype(BF16)


def each(count, body):
    def step(i, carry):
        body(i)
        return carry

    lax.fori_loop(0, count, step, 0)


def qkv_stage(x, gain, shift, w, bias, low, up, q, kv, red, red_out, normed):
    def norm(rows):
        normed[rows, :] = norm_low(x[rows, :], gain, shift)

    by_rows(x.shape[0], norm)
    keep(dot(normed[...], low[...], TURNED), red, red_out)

    def pair(j):
        made = dot(normed[...], w[j])
        for n in range(2):
            i = 2 * j + n
            mixed = made[:, n * 384 : (n + 1) * 384] + (bias[i] + dot(red[...], up[i]))
            q[i] = mixed[:, :128].astype(BF16)
            kv[i] = mixed[:, 128:].astype(BF16)

    each(NARROW // 2, pair)


def proj_stage(x, att, w, bias, low, up, gain, shift, low_up, mid, normed, red, red_out, red_up, red_up_out):
    keep(dot(att[...], low[...], TURNED), red, red_out)

    def part(rows):
        value = x[rows, :] + (dot(att[rows, :], w[...]) + bias + dot(red[rows, :], up[...]))
        mid[rows, :] = value
        normed[rows, :] = norm_low(value, gain, shift)

    by_rows(x.shape[0], part, 256)
    keep(dot(normed[...], low_up[...], TURNED), red_up, red_up_out)


def up_strip(i, normed, w, bias, red_up, up, active, slope):
    units = w.shape[2]
    cols = columns(i, units)
    value = dot(normed[...], w[i]) + (bias[i] + dot(red_up[...], up[:, cols]))
    made, made_slope = gelu_parts(value)
    active[:, cols] = made.astype(BF16)
    slope[:, cols] = made_slope.astype(BF16)


def down_stage(mid, active, w, bias, up, red, put):
    for n in range(mid.shape[1] // 256):
        cols = slice(n * 256, (n + 1) * 256)
        put(n, mid[:, cols] + (dot(active[...], w[:, cols]) + bias[:, cols] + dot(red[...], up[:, cols])))


def gelu_parts(x):
    square = x * x
    t = jnp.tanh(ROOT * (x + 0.044715 * (x * square)))
    half = 0.5 * (1.0 + t)
    slope = half + 0.5 * x * (1.0 - t * t) * (ROOT * (1.0 + 3 * 0.044715 * square))
    return x * half, slope


class Vectors:
    def __init__(self, ref, l):
        self.ref, self.l = ref, l

    def qkv(self, i):
        return self.ref[i, pl.ds(4 * self.l, 1), :384]

    def up(self, i):
        return self.ref[i, pl.ds(4 * self.l + 1, 1), :]

    def row(self, name):
        at = ("proj", "down", "gain1", "shift1", "gain2", "shift2").index(name)
        row, lane = 4 * self.l + 2 + at // 4, at % 4 * 128
        return jnp.concatenate([self.ref[i, row : row + 1, lane : lane + 128] for i in range(NARROW)], axis=1)


class Strips:
    def __init__(self, read):
        self.read = read

    def __getitem__(self, i):
        return self.read(i)


TABLES = ("low_qkv", "up_qkv", "low_proj", "up_proj", "low_up", "up_up", "low_down", "up_down")
SAVED = ("q", "kv", "peer", "att", "lse", "mid", "active", "slope", "x")


def task_list(layers):
    tasks = [("load", 0, 0, 3.0, None)]
    for l in range(layers):
        tasks.append(("qkv", l, 0, 7.0, ("qkv", l)))
        tasks += [("attend", l, n, 5.5, None) for n in range(2)]
        tasks.append(("proj", l, 0, 4.0, ("proj", l)))
        tasks += [("up", l, n, 6.0, ("up", l)) for n in range(2)]
        tasks.append(("down", l, 0, 5.0, ("down", l)))
    return tasks


class ForwardWork:
    def __init__(self, n_col, group, refs):
        self.__dict__.update(refs)
        self.group = group
        self.held = positions(group)
        self.r, self.c = lax.axis_index("row"), lax.axis_index("col")
        self.g = lax.rem(self.c, group)
        self.bias = pair_bias(self.held, self.g)
        self.layers = self.low_qkv.shape[0]

    def stage_copies(self, kind, l):
        full = self.full[kind]
        if kind == "qkv":
            pieces = []
            for i in range(NARROW):
                src = full.at[l, i]
                pieces.append((src, self.wq.at[i // 2, :, :, :, pl.ds(i % 2 * 384, 384)]))
            return pieces, self.wq
        if kind == "up":
            return [(full.at[l, i], self.wu.at[i]) for i in range(NARROW)], self.wu
        target = self.wp if kind == "proj" else self.wd
        return [(full.at[l, i], target.at[i]) for i in range(NARROW)], target

    def stage(self, kind, l):
        for src, dst in self.stage_copies(kind, l)[0]:
            pltpu.make_async_copy(src, dst, self.stage_sem.at[KINDS.index(kind)]).start()

    def staged(self, kind, l):
        target = self.stage_copies(kind, l)[1]
        pltpu.make_async_copy(target, target, self.stage_sem.at[KINDS.index(kind)]).wait()

    def save_copy(self, name, l):
        src = {
            "q": self.q, "kv": self.kv, "peer": self.peer.at[l], "att": self.att, "lse": self.lse,
            "mid": self.mid, "active": self.active, "slope": self.slope, "x": self.x,
        }[name]
        return pltpu.make_async_copy(src, self.saved[name].at[l], self.save_sem.at[l, SAVED.index(name)])

    def save(self, *names, l):
        for name in names:
            self.save_copy(name, l).start()

    def settled(self, *names, l):
        if l >= 0:
            for name in names:
                self.save_copy(name, l).wait()

    def result_copy(self, n):
        pair = pl.ds(2 * n, 2)
        return pltpu.make_async_copy(self.result.at[pair], self.out_result.at[pair], self.result_sem.at[n])

    def exchange(self, l, s):
        to = self.c - self.g + lax.rem(self.g + s, self.group)
        return pltpu.make_async_remote_copy(
            src_ref=self.kv, dst_ref=self.peer.at[l, s - 1],
            send_sem=self.kv_send.at[l, s - 1], recv_sem=self.kv_recv.at[l, s - 1],
            device_id=(self.r, to), device_id_type=MESH,
        )

    def run(self, name, l, part):
        vec = Vectors(self.vec, l)
        if name == "load":
            self.arrive_tokens()
            self.x[...] = self.tokens_v[...].astype(F32)
        elif name == "qkv":
            self.staged("qkv", l)
            self.settled("q", "kv", l=l - 1)
            if l > 0:
                for s in range(1, self.group):
                    self.exchange(l - 1, s).wait_send()
            w = self.wq.reshape(NARROW // 2, -1, 768)
            qkv_stage(
                self.x, vec.row("gain1"), vec.row("shift1"), w, Strips(vec.qkv), self.low_qkv.at[l],
                self.up_qkv.at[l], self.q, self.kv, self.red, self.reds.at[l, 0], self.normed,
            )
            for s in range(1, self.group):
                self.exchange(l, s).start()
            self.save("q", "kv", l=l)
        elif name == "attend":
            if part == 0:
                for s in range(1, self.group):
                    self.exchange(l, s).wait_recv()
                self.save("peer", l=l)
                self.settled("att", "lse", l=l - 1)
            kvs = [self.kv] + [self.peer.at[l, s - 1] for s in range(1, self.group)]
            size = NARROW // 2
            each(size, lambda n: attend_strip(self.held, self.bias, self.g, part * size + n, self.q, kvs, self.att, self.lse))
            if part == 1:
                self.save("att", "lse", l=l)
        elif name == "proj":
            self.staged("proj", l)
            self.settled("mid", l=l - 1)
            dim = self.att.shape[1]
            proj_stage(
                self.x, self.att, self.wp.reshape(dim, dim), vec.row("proj"), self.low_proj.at[l],
                self.up_proj.at[l], vec.row("gain2"), vec.row("shift2"), self.low_up.at[l],
                self.mid, self.normed, self.red, self.reds.at[l, 1], self.red_up, self.reds.at[l, 2],
            )
            self.save("mid", l=l)
        elif name == "up":
            if part == 0:
                self.staged("up", l)
                self.settled("active", "slope", l=l - 1)
            w = self.wu.reshape(NARROW, self.x.shape[1], -1)
            size = NARROW // 2
            each(size, lambda n: up_strip(
                part * size + n, self.normed, w, Strips(vec.up), self.red_up, self.up_up.at[l],
                self.active, self.slope,
            ))
            if part == 1:
                self.save("active", "slope", l=l)
                keep(dot(self.active[...], self.low_down[l], TURNED), self.red, self.reds.at[l, 3])
        elif name == "down":
            self.staged("down", l)
            self.settled("x", l=l - 1)
            dim = self.x.shape[1]

            def put(n, value):
                if l < self.layers - 1:
                    self.x[:, columns(n, 256)] = value
                else:
                    for m in range(2):
                        self.result[2 * n + m] = value[:, m * 128 : (m + 1) * 128].astype(BF16)
                    self.result_copy(n).start()

            down_stage(
                self.mid, self.active, self.wd.reshape(-1, dim), vec.row("down"), self.up_down.at[l], self.red, put,
            )
            if l < self.layers - 1:
                self.save("x", l=l)

    def close(self):
        last = self.layers - 1
        self.settled(*[name for name in SAVED if name not in ("x", "peer")], l=last)
        for l in range(self.layers):
            self.settled("peer", l=l)
        for s in range(1, self.group):
            self.exchange(last, s).wait_send()
        for n in range(NARROW // 2):
            self.result_copy(n).wait()


def gather_body(n_row, n_col, layers, group, names, *refs):
    refs = dict(zip(names, refs))
    shard = {kind: refs["shard_" + kind] for kind in KINDS}
    full = {kind: refs["full_" + kind] for kind in KINDS}
    tokens, cotangent, vector = refs["tokens"], refs["cotangent"], refs["vector"]
    own_tokens, own_cotangent, vectors = refs["own_tokens"], refs["own_cotangent"], refs["vectors"]
    local_sem, send_sem, recv_sem = refs["local_sem"], refs["send_sem"], refs["recv_sem"]
    near_sem, out_sem, in_sem = refs["near_sem"], refs["out_sem"], refs["in_sem"]
    r = lax.axis_index("row")
    c = lax.axis_index("col")
    link_bits = [b for b in (2**k for k in range(1, 8)) if b < n_col]
    depth = shard["up"].shape[1]

    def row_peer(s):
        return (lax.rem(r + s, n_row), c)

    def col_peer(bit):
        return (r, c ^ bit)

    peers = [row_peer(s) for s in range(1, n_row)]
    peers += [(r, lax.rem(c + d, n_col)) for d in range(1, n_col)]
    barrier = pltpu.get_barrier_semaphore()
    for peer in peers:
        pl.semaphore_signal(barrier, inc=1, device_id=peer, device_id_type=MESH)
    pl.semaphore_wait(barrier, len(peers))

    per, width = BLOCKS // group, tokens.shape[1]

    def own_place(ref, b, col):
        if len(ref.shape) == 2:
            start = pl.multiple_of(col * width, width)
            return ref.at[pl.ds(b * BLOCK, BLOCK), pl.ds(start, width)]
        return ref.at[col, pl.ds(b * BLOCK, BLOCK)]

    def from_place(ref, b, col):
        start = (col // group) * LEN + place_of(group, lax.rem(col, group), b) * BLOCK
        return ref.at[pl.ds(pl.multiple_of(start, BLOCK), BLOCK)]

    exchanged = ((tokens, own_tokens), (cotangent, own_cotangent))

    def near(n, b):
        src, dst = exchanged[n]
        return pltpu.make_async_copy(from_place(src, b, c), own_place(dst, b, c), near_sem.at[n * per + b])

    def near_vector():
        return pltpu.make_async_copy(vector, vectors.at[c], near_sem.at[2 * per])

    def far(src, dst, n, peer):
        return pltpu.make_async_remote_copy(
            src_ref=src, dst_ref=dst, send_sem=out_sem.at[n], recv_sem=in_sem.at[n],
            device_id=peer, device_id_type=MESH,
        )

    def start_exchange(n):
        src, dst = exchanged[n]
        for b in range(per):
            near(n, b).start()
        for d in range(1, n_col):
            to = lax.rem(c + d, n_col)
            for b in range(per):
                far(from_place(src, b, to), own_place(dst, b, c), n, (r, to)).start()

    def wait_exchange(n):
        _, dst = exchanged[n]
        for b in range(per):
            near(n, b).wait()
        if len(dst.shape) == 2:
            ref = dst.at[:, pl.ds(0, (n_col - 1) * width)]
        else:
            ref = dst.at[pl.ds(0, n_col - 1)]
        far(ref, ref, n, col_peer(1)).wait()

    def own(kind, l, h, dst):
        ref = shard[kind]
        size = ref.shape[-2] // CUTS[kind]
        if len(ref.shape) == 3:
            return [(ref.at[l, pl.ds(h * size, size)], dst)]
        return [
            (ref.at[l, n, pl.ds(h * size, size)], dst.at[:, pl.ds(n * ref.shape[3], ref.shape[3])])
            for n in range(ref.shape[1])
        ]

    def block(kind, l, h, row, col):
        if kind in ("qkv", "up"):
            return full[kind].at[l, col, row, h]
        start = pl.multiple_of(row * depth, depth)
        return full[kind].at[l, col, h, :, pl.ds(start, depth)]

    def strip(kind, l, h, col):
        if kind in ("qkv", "up"):
            return full[kind].at[l, col, :, h]
        return full[kind].at[l, col, h]

    def amount(kind, l, h, strips, rows):
        if kind in ("qkv", "up"):
            return full[kind].at[l, pl.ds(0, strips), pl.ds(0, rows), h]
        return full[kind].at[l, pl.ds(0, strips), h, :, pl.ds(0, rows * depth)]

    chunks = []
    for l in range(layers):
        for kind in KINDS:
            for h in range(CUTS[kind]):
                order = []
                for d in ORDERS[l % len(ORDERS)][kind][h // 2][h % 2]:
                    if d == "z":
                        order.append("z")
                    elif d < len(link_bits):
                        order.append(link_bits[d])
                order += link_bits[2:]
                chunks.append((kind, l, h, tuple(order)))
    phases = len(link_bits) + n_row - 1

    def remote(src, dst, k, p, peer, way=0):
        at = (k * (phases + 1) + p) * 2 + way
        return pltpu.make_async_remote_copy(
            src_ref=src, dst_ref=dst, send_sem=send_sem.at[at], recv_sem=recv_sem.at[at],
            device_id=peer, device_id_type=MESH,
        )

    def plan(k):
        return transfer_plan(chunks[k][3], n_row)

    def ways(hop):
        return (
            (r - hop + 1, (r - hop + 1 >= 0) & (r + 1 < n_row), r - hop >= 0, 1),
            (r + hop - 1, (r + hop - 1 < n_row) & (r >= 1), r + hop < n_row, n_row - 1),
        )

    def local_start(k):
        kind, l, h, _ = chunks[k]
        for src, dst in own(kind, l, h, block(kind, l, h, r, c)):
            pltpu.make_async_copy(src, dst, local_sem.at[k]).start()

    def local_wait(k):
        kind, l, h, _ = chunks[k]
        ref = block(kind, l, h, r, c)
        pltpu.make_async_copy(ref, ref, local_sem.at[k]).wait()

    def issue(k, p):
        kind, l, h, order = chunks[k]
        d, masks, rows = plan(k)[p]

        def send(m, row, first, peer, way):
            dst = block(kind, l, h, row, c ^ m)
            for src, to in own(kind, l, h, dst) if m == 0 and first else [(dst, dst)]:
                remote(src, to, k, p, peer, way).start()

        if isinstance(d, tuple):
            for way, (row, goes, _, step) in enumerate(ways(d[1])):

                @pl.when(goes)
                def _():
                    for m in masks:
                        send(m, row, d[1] == 1, row_peer(step), way)

            return
        for m in masks:
            if rows:
                ref = strip(kind, l, h, c ^ m)
                remote(ref, ref, k, p, col_peer(d)).start()
            else:
                send(m, r, True, col_peer(d), 0)

    def moved(k, p, send):
        kind, l, h, order = chunks[k]
        d, masks, rows = plan(k)[p]
        ref = amount(kind, l, h, len(masks), n_row if rows else 1)
        if not isinstance(d, tuple):
            copy = remote(ref, ref, k, p, col_peer(1))
            copy.wait_send() if send else copy.wait_recv()
            return
        for way, (_, goes, comes, step) in enumerate(ways(d[1])):

            @pl.when(goes if send else comes)
            def _():
                copy = remote(ref, ref, k, p, row_peer(step), way)
                copy.wait_send() if send else copy.wait_recv()

    def share(k, p):
        kind, l, h, order = chunks[k]
        (d, masks, _), (_, later, rows) = plan(k)[p : p + 2]
        if not rows:
            return
        fresh = masks if isinstance(d, tuple) else later[len(masks):]
        for m in fresh:
            ref = strip(kind, l, h, c ^ m)
            remote(ref, ref, k, phases, col_peer(1)).start()

    def shared(k):
        kind, l, h, _ = chunks[k]
        ref = amount(kind, l, h, n_col // 2, n_row)
        return remote(ref, ref, k, phases, col_peer(1))

    def finish(k, p):
        moved(k, p, False)
        if plan(k)[p][0] == ("z", n_row - 1):
            local_wait(k)
        share(k, p)

    count = len(chunks)
    near_vector().start()
    for d in range(1, n_col):
        far(vector, vectors.at[c], 2, (r, lax.rem(c + d, n_col))).start()
    start_exchange(0)
    for k in range(count):
        local_start(k)
    def vectors_arrive():
        near_vector().wait()
        rest = vectors.at[pl.ds(0, n_col - 1)]
        far(rest, rest, 2, col_peer(1)).wait()

    work = None
    if "x" in refs:
        refs.update(full=full, saved={name: refs["saved_" + name] for name in SAVED})

        loads = [(refs["in_" + name], refs[name]) for name in TABLES]
        loads += [(own_tokens, refs["tokens_v"]), (vectors, refs["vec"])]
        loads = [pltpu.make_async_copy(s, d, refs["load_sem"].at[n]) for n, (s, d) in enumerate(loads)]
        for copy in loads[: len(TABLES)]:
            copy.start()

        def arrive_tokens():
            vectors_arrive()
            wait_exchange(0)
            for copy in loads[len(TABLES) :]:
                copy.start()
            for copy in loads:
                copy.wait()

        refs.update(arrive_tokens=arrive_tokens)
        work = ForwardWork(n_col, group, refs)

    pieces = []
    for kind, l, h, order in chunks:
        size = 2 * math.prod(shard[kind].shape[1:]) // CUTS[kind]
        pieces.append(((kind, l), order, size))
    ops = transfer_schedule(pieces, n_row, task_list(layers) if work else [])
    quiet = max(n for n, (op, _, _) in enumerate(ops) if op == "wait")
    for n, (op, k, p) in enumerate(ops):
        if op == "start":
            issue(k, p)
        elif op == "wait":
            finish(k, p)
        elif op == "stage":
            for at, (kind, l, _, _) in enumerate(chunks):
                if (kind, l) == (k, p):
                    shared(at).wait_recv()
            work.stage(k, p)
        else:
            work.run(k, *p)
        if n == quiet:
            start_exchange(1)
    for k in range(count):
        for p in range(phases):
            moved(k, p, True)
        shared(k).wait_send()
        if not work:
            shared(k).wait_recv()
    if work:
        work.close()
    else:
        vectors_arrive()
        wait_exchange(0)
    wait_exchange(1)


def gather_inputs(n_row, n_col, group, qkv, proj, up, down, tokens, cotangent, vector, tables=None):
    layers, depth = up.shape[0], up.shape[1]
    width, units = proj.shape[1], down.shape[1]
    dim, hidden = depth * n_row, units * n_col
    mine = LEN // group
    cuts = [CUTS[kind] for kind in KINDS]
    own = (mine, dim) if width % 128 == 0 else (n_col, mine, width)
    hbm = pl.BlockSpec(memory_space=pltpu.HBM)
    vmem = pl.BlockSpec(memory_space=pltpu.VMEM)
    dma = pltpu.SemaphoreType.DMA
    count = layers * sum(cuts)
    phases = n_col.bit_length() + n_row - 2
    inputs = [("shard_" + kind, array, hbm) for kind, array in zip(KINDS, (qkv, proj, up, down))]
    inputs += [("tokens", tokens, hbm), ("cotangent", cotangent, hbm), ("vector", vector, hbm)]
    outputs = [
        ("full_qkv", (layers, n_col, n_row, cuts[0], depth // cuts[0], 3 * width), BF16, hbm),
        ("full_proj", (layers, n_col, cuts[1], width // cuts[1], dim), BF16, hbm),
        ("full_up", (layers, n_col, n_row, cuts[2], depth // cuts[2], units), BF16, hbm),
        ("full_down", (layers, n_col, cuts[3], units // cuts[3], dim), BF16, hbm),
        ("own_tokens", own, BF16, hbm),
        ("own_cotangent", own, BF16, hbm),
        ("vectors", (n_col,) + vector.shape, F32, hbm),
    ]
    scratch = [
        ("local_sem", dma((count,))),
        ("send_sem", dma((count * phases * 2,))),
        ("recv_sem", dma((count * phases * 2,))),
        ("near_sem", dma((2 * (BLOCKS // group) + 1,))),
        ("out_sem", dma((3,))),
        ("in_sem", dma((3,))),
    ]
    if tables is not None:
        rank = tables[0].shape[1]
        inputs += [("in_" + name, table, hbm) for name, table in zip(TABLES, tables)]
        strip = (NARROW, mine)
        kept = {
            "q": (strip + (128,), BF16), "kv": (strip + (256,), BF16), "att": ((mine, dim), BF16),
            "lse": ((NARROW, 8, mine), F32), "mid": ((mine, dim), F32), "active": ((mine, hidden), BF16),
            "slope": ((mine, hidden), BF16),
            "x": ((mine, dim), F32), "peer": ((group - 1,) + strip + (256,), BF16),
        }
        outputs += [("saved_" + name, (layers,) + kept[name][0], kept[name][1], hbm) for name in SAVED]
        outputs += [
            ("reds", (layers, 4, rank, mine), BF16, vmem),
            ("out_result", (NARROW, mine, 128), BF16, hbm),
        ]
        scratch += [
            (name, pltpu.VMEM(((layers,) if name == "peer" else ()) + kept[name][0], kept[name][1]))
            for name in SAVED
        ]
        scratch += [
            *[(name, pltpu.VMEM(table.shape, table.dtype)) for name, table in zip(TABLES, tables)],
            ("wq", pltpu.VMEM((NARROW // 2, n_row, cuts[0], depth // cuts[0], 768), BF16)),
            ("wp", pltpu.VMEM((NARROW, cuts[1], width // cuts[1], dim), BF16)),
            ("wu", pltpu.VMEM((NARROW, n_row, cuts[2], depth // cuts[2], units), BF16)),
            ("wd", pltpu.VMEM((NARROW, cuts[3], units // cuts[3], dim), BF16)),
            ("tokens_v", pltpu.VMEM((mine, dim), BF16)),
            ("normed", pltpu.VMEM((mine, dim), BF16)),
            ("red", pltpu.VMEM((mine, rank), BF16)),
            ("red_up", pltpu.VMEM((mine, rank), BF16)),
            ("vec", pltpu.VMEM((n_col,) + vector.shape, F32)),
            ("stage_sem", dma((4,))),
            ("save_sem", dma((layers, len(SAVED)))),
            ("kv_send", dma((layers, group - 1))),
            ("kv_recv", dma((layers, group - 1))),
            ("load_sem", dma((2 + len(TABLES),))),
            ("result", pltpu.VMEM((NARROW, mine, 128), BF16)),
            ("result_sem", dma((NARROW // 2,))),
        ]
    names = [x[0] for x in inputs] + [x[0] for x in outputs] + [x[0] for x in scratch]
    outs = pl.pallas_call(
        functools.partial(gather_body, n_row, n_col, layers, group, tuple(names)),
        out_shape=[jax.ShapeDtypeStruct(shape, kind) for _, shape, kind, _ in outputs],
        in_specs=[spec for _, _, spec in inputs],
        out_specs=[spec for _, _, _, spec in outputs],
        scratch_shapes=[shape for _, shape in scratch],
        compiler_params=pltpu.CompilerParams(
            collective_id=0, has_side_effects=True, vmem_limit_bytes=60 * 2**20
        ),
        name="gather_inputs",
    )(*[array for _, array, _ in inputs])
    outs = dict(zip([x[0] for x in outputs], outs))

    merge = 128 // width
    strips = n_col // merge
    qkv_full = outs["full_qkv"].reshape(layers, n_col, dim, 3 * width)
    up_full = outs["full_up"].reshape(layers, n_col, dim, units)
    rows, vec = [outs["own_tokens"], outs["own_cotangent"]], outs["vectors"]
    if merge > 1:
        qkv_full = qkv_full.reshape(layers, strips, merge, dim, 3, width).transpose(0, 1, 3, 4, 2, 5)
        up_full = up_full.reshape(layers, strips, merge, dim, units).transpose(0, 1, 3, 2, 4)
        rows = [x.transpose(1, 0, 2).reshape(mine, dim) for x in rows]
        vec = vec.reshape(strips, merge, layers, 4, 4 * 128)
        first = vec[:, :, :, 0, : 3 * width].reshape(strips, merge, layers, 3, width).transpose(0, 2, 3, 1, 4)
        first = jnp.pad(first.reshape(strips, layers, 384), ((0, 0), (0, 0), (0, 128)))
        second = vec[:, :, :, 1, :units].transpose(0, 2, 1, 3).reshape(strips, layers, 512)
        rest = vec[:, :, :, 2:, : 4 * width].reshape(strips, merge, layers, 2, 4, width)
        rest = rest.transpose(0, 2, 3, 4, 1, 5).reshape(strips, layers, 2, 512)
        vec = jnp.concatenate([first[:, :, None], second[:, :, None], rest], axis=2)
        vec = vec.reshape(strips, layers * 4, 512)
    outs.update(
        qkv=qkv_full.reshape(layers, strips, dim, 384),
        proj=outs["full_proj"].reshape(layers, dim, dim),
        up=up_full.reshape(layers, strips, dim, units * merge),
        down=outs["full_down"].reshape(layers, hidden, dim),
        tokens=rows[0], cotangent=rows[1], vec=vec, result=outs.get("out_result"),
    )
    return outs


PARAMS = pltpu.CompilerParams(vmem_limit_bytes=60 * 2**20)


def shape_of(shape, kind):
    return jax.ShapeDtypeStruct(shape, kind)


def kernel(body, name, inputs, outputs, scratch=()):
    spaces = (pl.BlockSpec(memory_space=pltpu.VMEM), pl.BlockSpec(memory_space=pltpu.HBM))
    return pl.pallas_call(
        body,
        out_shape=[shape_of(shape, kind) for shape, kind, _ in outputs],
        in_specs=[spaces[far] for _, far in inputs],
        out_specs=[spaces[far] for _, _, far in outputs],
        scratch_shapes=list(scratch),
        compiler_params=PARAMS,
        name=name,
    )(*[array for array, _ in inputs])


def own_group(group):
    return lax.rem(lax.axis_index("col"), group)


def qkv_body(l, x, vec, w, low, up, q, kv, red_out, red, normed, buf, sem):
    copies = []
    for i in range(NARROW):
        copies.append(pltpu.make_async_copy(w.at[l, i], buf.at[i // 2, :, columns(i % 2, 384)], sem.at[i]))
        copies[-1].start()
    for copy in copies:
        copy.wait()
    v = Vectors(vec, l)
    qkv_stage(x, v.row("gain1"), v.row("shift1"), buf, Strips(v.qkv), low.at[l], up.at[l], q, kv, red, red_out, normed)


def qkv_kernel(l, x, vec, w, low, up):
    tokens, dim = x.shape
    return kernel(
        functools.partial(qkv_body, l), "qkv",
        [(x, False), (vec, False), (w, True), (low, False), (up, False)],
        [((NARROW, tokens, 128), BF16, False), ((NARROW, tokens, 256), BF16, False), ((low.shape[1], tokens), BF16, False)],
        [pltpu.VMEM((tokens, low.shape[1]), BF16), pltpu.VMEM((tokens, dim), BF16), pltpu.VMEM((NARROW // 2, dim, 768), BF16), pltpu.SemaphoreType.DMA((NARROW,))],
    )


def attend_body(group, g_ref, q, *refs):
    held = positions(group)
    kvs, (out, lse) = refs[:group], refs[group:]
    bias = pair_bias(held, g_ref[0])
    each(NARROW, lambda i: attend_strip(held, bias, g_ref[0], i, q, kvs, out, lse))


def attend_kernel(group, g, q, kvs):
    tokens = q.shape[1]
    return pl.pallas_call(
        functools.partial(attend_body, group),
        out_shape=[shape_of((tokens, NARROW * 128), BF16), shape_of((NARROW, 8, tokens), F32)],
        in_specs=[pl.BlockSpec(memory_space=pltpu.SMEM)] + [pl.BlockSpec(memory_space=pltpu.VMEM)] * (group + 1),
        out_specs=[pl.BlockSpec(memory_space=pltpu.VMEM)] * 2,
        compiler_params=PARAMS,
        name="attend",
    )(g, q, *kvs)


def mlp_body(l, x, att, vec, wp, wu, wd, *refs):
    low_proj, up_proj, low_up, up_up, low_down, up_down = [ref.at[l] for ref in refs[:6]]
    mid, result, active, slope, reds, red, red_up, normed, bp, bu, bd, sem = refs[6:]
    copies = []
    for n, (src, dst) in enumerate(((wp.at[l], bp), (wu.at[l], bu), (wd.at[l], bd))):
        copies.append(pltpu.make_async_copy(src, dst, sem.at[n]))
        copies[-1].start()
    v = Vectors(vec, l)
    copies[0].wait()
    proj_stage(
        x, att, bp, v.row("proj"), low_proj, up_proj, v.row("gain2"), v.row("shift2"), low_up,
        mid, normed, red, reds.at[0], red_up, reds.at[1],
    )
    copies[1].wait()
    each(NARROW, lambda i: up_strip(i, normed, bu, Strips(v.up), red_up, up_up, active, slope))
    copies[2].wait()

    def put(n, value):
        if len(result.shape) == 2:
            result[:, columns(n, 256)] = value
        else:
            for m in range(2):
                result[2 * n + m] = value[:, m * 128 : (m + 1) * 128].astype(BF16)

    keep(dot(active[...], low_down[...], TURNED), red, reds.at[2])
    down_stage(mid, active, bd, v.row("down"), up_down, red, put)


def mlp_kernel(l, final, x, att, vec, wp, wu, wd, tables):
    tokens, dim = x.shape
    hidden = wd.shape[1]
    rank = tables[0].shape[1]
    result = ((NARROW, tokens, 128), BF16, False) if final else ((tokens, dim), F32, False)
    return kernel(
        functools.partial(mlp_body, l), "mlp",
        [(x, False), (att, False), (vec, False), (wp, True), (wu, True), (wd, True)] + [(t, False) for t in tables],
        [((tokens, dim), F32, False), result] + [((tokens, hidden), BF16, False)] * 2 + [((3, rank, tokens), BF16, False)],
        [
            pltpu.VMEM((tokens, rank), BF16), pltpu.VMEM((tokens, rank), BF16),
            pltpu.VMEM((tokens, dim), BF16), pltpu.VMEM(wp.shape[1:], BF16),
            pltpu.VMEM(wu.shape[1:], BF16), pltpu.VMEM(wd.shape[1:], BF16), pltpu.SemaphoreType.DMA((3,)),
        ],
    )


def mlp_back_stage(vec, grad, active, g_hid, mid, att, low, total, wp, wu, wd, reds, t, grads, g_mid, waits, strip_waits):
    low[...] = grad[...].astype(BF16)
    g_red = dot(low[...], t["up_down"], TURNED).astype(BF16)
    rank = g_red.shape[1]
    units = wu.shape[2]
    total[...] = jnp.zeros_like(total)

    def strip(i):
        cols = columns(i, units)
        strip_waits(i)
        g_active = dot(low[...], wd[cols, :], TURNED) + dot(g_red, t["low_down"][:, cols])
        g_hid[:, cols] = (g_active * g_hid[:, cols].astype(F32)).astype(BF16)
        total[...] += dot(g_hid[:, cols], wu[i], TURNED)

    each(NARROW, strip)

    def give(at, value):
        size = value.shape[1] // NARROW
        for i in range(NARROW):
            grads[i, :, at : at + size] = value[:, i * size : (i + 1) * size].astype(BF16)

    give(384 + 2 * units, dot(reds[3], low[...]))
    give(384 + units, dot(g_red, active[...], CROSS))
    give(384, dot(reds[2], g_hid[...]))
    g_hid[:, :rank] = dot(g_hid[...], t["up_up"][...], TURNED).astype(BF16)
    waits("mid")
    gain, shift = vec.row("gain2"), vec.row("shift2")
    dim = mid.shape[1]

    def norm(rows):
        scaled, inverse = norm_parts(mid[rows, :])
        active[rows, :dim] = (scaled * gain + shift).astype(BF16)
        g_normed = total[rows, :] + dot(g_hid[rows, :rank], t["low_up"])
        value = grad[rows, :] + norm_grad(g_normed, scaled, inverse, gain)
        g_mid[rows, :] = value
        low[rows, :] = value.astype(BF16)

    by_rows(mid.shape[0], norm)
    give(256, dot(g_hid[:, :rank], active[:, :dim], CROSS))
    give(128, dot(reds[1], low[...]))
    g_red_proj = dot(low[...], t["up_proj"], TURNED).astype(BF16)
    waits("att")
    waits("proj")
    give(0, dot(g_red_proj, att[...], CROSS))
    low[...] = (dot(low[...], wp[...], TURNED) + dot(g_red_proj, t["low_proj"])).astype(BF16)


def qkv_back_stage(vec, x, g_mid, gq, parts, total, g_red, normed, wq, red, low, up, grads, put, waits, done=None):
    waits("gq")
    waits("qkv")
    rank, tokens = red.shape
    small = jnp.zeros((tokens, rank), F32)

    def mixed(i, rows):
        return jnp.concatenate([gq[i, rows, :], parts[0][i, rows, :]], axis=1)

    def product(j, rows):
        made = dot(jnp.concatenate([mixed(2 * j, rows), mixed(2 * j + 1, rows)], axis=1), wq[j], TURNED)
        total[rows, :] = made if j == 0 else total[rows, :] + made

    every = pl.ds(0, tokens)
    for j in range(NARROW // 2):
        for i in (2 * j, 2 * j + 1):
            waits(("part", i))
            parts[0][i] = sum(part[i].astype(F32) for part in parts).astype(BF16)
            g_mixed = mixed(i, every)
            grads[i, :, 128:512] = dot(red[...], g_mixed).astype(BF16)
            small = small + dot(g_mixed, up[i], TURNED)
        if not done:
            product(j, every)
    g_low_rank = small.astype(BF16)
    g_red[...] = g_low_rank
    waits("x")
    waits("g_mid")
    gain, shift = vec.row("gain1"), vec.row("shift1")

    def norm(rows):
        scaled, inverse = norm_parts(x[rows, :].astype(F32))
        normed[rows, :] = (scaled * gain + shift).astype(BF16)
        g_normed = total[rows, :] + dot(g_red[rows, :], low[...])
        put(rows, g_mid[rows, :] + norm_grad(g_normed, scaled, inverse, gain))

    def lower():
        g_low = dot(g_low_rank, normed[...], CROSS).astype(BF16)
        for i in range(NARROW):
            grads[i, :, :128] = g_low[:, i * 128 : (i + 1) * 128]

    if not done:
        by_rows(tokens, norm)
        lower()
        return

    def first_norm(rows):
        normed[rows, :] = norm_low(x[rows, :].astype(F32), gain, shift)

    by_rows(tokens, first_norm)
    lower()
    done(-1)
    for b in range(tokens // BLOCK):
        for j in range(NARROW // 2):
            product(j, pl.ds(b * BLOCK, BLOCK))
        for n in range(2):
            norm(pl.ds(b * BLOCK + n * BLOCK // 2, BLOCK // 2))
        done(b)


def back_body(lq, lm, group, names, *refs):
    R = dict(zip(names, refs))
    held = positions(group)
    sem, started = R["sem"], {}

    def waits(name):
        for copy in started.pop(name, ()):
            copy.wait()

    count = [0]

    def begin(name, *copies):
        started[name] = []
        for src, dst in copies:
            copy = pltpu.make_async_copy(src, dst, sem.at[count[0]])
            count[0] += 1
            copy.start()
            started[name].append(copy)

    def strip_copies(l, i, base):
        cols = columns(i, R["wu"].shape[2])
        pairs = (
            (R["slopes"].at[l, :, cols], R["g_hid"].at[:, cols]), (R["actives"].at[l, :, cols], R["active"].at[:, cols]),
            (R["w_down"].at[l, cols], R["wd"].at[cols]), (R["w_up"].at[l, i], R["wu"].at[i]),
        )
        return [pltpu.make_async_copy(src, dst, sem.at[base + 4 * i + n]) for n, (src, dst) in enumerate(pairs)]

    strip_base = {}

    def load_strips(l):
        strip_base[l] = count[0]
        count[0] += 4 * NARROW
        for i in range(NARROW):
            for copy in strip_copies(l, i, strip_base[l]):
                copy.start()

    def strip_waits(l):
        def wait(i):
            for copy in strip_copies(l, i, strip_base[l]):
                copy.wait()

        return wait

    if lq is not None:
        begin("gq", (R["in_gq"], R["gq"]), *[(R["in_part%d" % j], R["part%d" % j]) for j in range(group)])
        begin("qkv", *[
            (R["w_qkv"].at[lq, i], R["wq"].at[i // 2, :, columns(i % 2, 384)]) for i in range(NARROW)
        ])
        begin("x", (R["in_x"], R["x"]))
        begin("g_mid", (R["in_g_mid"], R["total2"]))
    else:
        begin("cotangent", (R["cotangent"], R["low"]))
    if lm is not None:
        load_strips(lm)
        begin("proj", (R["w_proj"].at[lm], R["wp"]))
        begin("att", (R["atts"].at[lm], R["att"]))
        begin("kv", (R["kvs"].at[lm], R["kv"]), (R["peers"].at[lm], R["peer"]), (R["lses"].at[lm], R["lse"]))
    if lq is not None:
        vec = Vectors(R["vec"], lq)

        def put(rows, value):
            if lm is None:
                for i in range(NARROW):
                    R["out"][i, rows, :] = value[:, i * 128 : (i + 1) * 128].astype(BF16)
            else:
                R["grad"][rows, :] = value

        qkv_back_stage(
            vec, R["x"], R["total2"], R["gq"], [R["part%d" % j] for j in range(group)], R["total"],
            R["g_red"], R["low"], R["wq"],
            R["reds"].at[lq, 0], R["low_qkv"].at[lq], R["up_qkv"].at[lq], R["grads_qkv"], put, waits,
        )
    else:
        waits("cotangent")
        R["grad"][...] = R["low"][...].astype(F32)
    if lm is None:
        return
    begin("q", (R["qs"].at[lm], R["gq"]))
    begin("mid", (R["mids"].at[lm], R["x" if lq is not None and R["x"].dtype == F32 else "mid"]))
    mid = R["x" if lq is not None and R["x"].dtype == F32 else "mid"]
    t = {name: R[name].at[lm] for name in TABLES}
    vec = Vectors(R["vec"], lm)
    mlp_back_stage(
        vec, R["grad"], R["active"], R["g_hid"], mid, R["att"], R["low"], R["total"], R["wp"], R["wu"], R["wd"],
        R["reds"].at[lm], {k: (v if k in ("low_down", "up_up") else v[...]) for k, v in t.items() if "qkv" not in k},
        R["grads_mlp"], R["total2"], waits, strip_waits(lm),
    )
    out_mid = pltpu.make_async_copy(R["total2"], R["out_g_mid"], sem.at[count[0]])
    out_mid.start()
    waits("q")
    waits("kv")
    bias = pair_bias(held, R["g"][0])
    kvs = [R["kv"]] + [R["peer"].at[j] for j in range(group - 1)]
    gkvs = [R["part%d" % j] for j in range(group)]
    each(NARROW, lambda i: attend_back_strip(
        held, bias, R["g"][0], i, R["gq"], R["lse"], R["att"], R["low"], kvs, R["gq"], gkvs
    ))
    outs = [(R["gq"], R["out_gq"])] + [(R["part%d" % j], R["out_part%d" % j]) for j in range(group)]
    copies = [pltpu.make_async_copy(src, dst, sem.at[count[0] + 1 + n]) for n, (src, dst) in enumerate(outs)]
    for copy in copies:
        copy.start()
    for copy in copies:
        copy.wait()
    out_mid.wait()


def back_kernel(lq, lm, group, g, outs, tables, carried):
    layers, _, dim, _ = outs["qkv"].shape
    hidden = outs["down"].shape[1]
    tokens = outs["tokens"].shape[0]
    rank = tables[0].shape[1]
    strip = (NARROW, tokens)
    inputs = [("g", g, pl.BlockSpec(memory_space=pltpu.SMEM))]
    near, far = pl.BlockSpec(memory_space=pltpu.VMEM), pl.BlockSpec(memory_space=pltpu.HBM)
    inputs += [(name, table, near) for name, table in zip(TABLES, tables)]
    inputs += [("vec", outs["vec"], near), ("reds", outs["reds"], near)]
    outputs, scratch = [], []

    def vmem(name, shape, kind):
        scratch.append((name, pltpu.VMEM(shape, kind)))

    vmem("gq", strip + (128,), BF16)
    for j in range(group):
        vmem("part%d" % j, strip + (256,), BF16)
    vmem("total", (tokens, dim), F32)
    vmem("total2", (tokens, dim), F32)
    vmem("low", (tokens, dim), BF16)
    if lq is not None:
        g_mid, gq, parts = carried
        x = outs["tokens"] if lq == 0 else outs["saved_x"][lq - 1]
        inputs += [("in_gq", gq, far), ("in_g_mid", g_mid, far), ("in_x", x, far), ("w_qkv", outs["qkv"], far)]
        inputs += [("in_part%d" % j, part, far) for j, part in enumerate(parts)]
        vmem("wq", (NARROW // 2, dim, 768), BF16)
        vmem("g_red", (tokens, rank), BF16)
        vmem("x", (tokens, dim), x.dtype)
        outputs.append(("grads_qkv", (NARROW, rank, 512), BF16, near))
        if lm is None:
            outputs.append(("out", strip + (128,), BF16, near))
    if lm is not None:
        if lq is None:
            inputs.append(("cotangent", outs["cotangent"], far))
        for name in ("active", "slope", "mid", "att", "q", "kv", "peer", "lse"):
            inputs.append((name + "s", outs["saved_" + name], far))
        inputs += [("w_" + name, outs[name], far) for name in ("proj", "up", "down")]
        vmem("wp", (dim, dim), BF16)
        vmem("wu", (NARROW, dim, hidden // NARROW), BF16)
        vmem("wd", (hidden, dim), BF16)
        vmem("grad", (tokens, dim), F32)
        if lq is None or x.dtype != F32:
            vmem("mid", (tokens, dim), F32)
        vmem("att", (tokens, dim), BF16)
        vmem("active", (tokens, hidden), BF16)
        vmem("g_hid", (tokens, hidden), BF16)
        vmem("kv", strip + (256,), BF16)
        vmem("peer", (group - 1,) + strip + (256,), BF16)
        vmem("lse", (NARROW, 8, tokens), F32)
        outputs.append(("grads_mlp", (NARROW, rank, 512 + 2 * hidden // NARROW), BF16, near))
        outputs += [("out_g_mid", (tokens, dim), F32, far), ("out_gq", strip + (128,), BF16, far)]
        outputs += [("out_part%d" % j, strip + (256,), BF16, far) for j in range(group)]
    scratch.append(("sem", pltpu.SemaphoreType.DMA((96,))))
    names = [x[0] for x in inputs] + [x[0] for x in outputs] + [x[0] for x in scratch]
    made = pl.pallas_call(
        functools.partial(back_body, lq, lm, group, tuple(names)),
        out_shape=[shape_of(shape, kind) for _, shape, kind, _ in outputs],
        in_specs=[spec for _, _, spec in inputs],
        out_specs=[spec for _, _, _, spec in outputs],
        scratch_shapes=[shape for _, shape in scratch],
        compiler_params=PARAMS,
        name="back",
    )(*[array for _, array, _ in inputs])
    return dict(zip([x[0] for x in outputs], made))


SITES = {"mlp": (1, 1, 2, 2, 3, 3), "qkv": (0, 0)}


def backward_body(layers, group, n_row, n_col, names, *refs):
    R = dict(zip(names, refs))
    held = positions(group)
    per = BLOCKS // group
    r, c = lax.axis_index("row"), lax.axis_index("col")
    g = lax.rem(c, group)
    seqs = n_col // group
    tokens = per * BLOCK
    bias = pair_bias(held, g)

    def row_peer(s):
        return (lax.rem(r + s, n_row), c)

    def col_peer(d):
        return lax.rem(c + d, n_col)

    peers = [row_peer(s) for s in range(1, n_row)] + [(r, col_peer(d)) for d in range(1, n_col)]
    barrier = pltpu.get_barrier_semaphore()
    for peer in peers:
        pl.semaphore_signal(barrier, inc=1, device_id=peer, device_id_type=MESH)
    pl.semaphore_wait(barrier, len(peers))

    sem, started, count = R["sem"], {}, [0]

    def begin(name, *copies):
        started[name] = []
        for src, dst in copies:
            copy = pltpu.make_async_copy(src, dst, sem.at[count[0]])
            count[0] += 1
            copy.start()
            started[name].append(copy)

    def waits(name):
        for copy in started.pop(name, ()):
            copy.wait()

    def strip_copies(l, i, base):
        cols = columns(i, R["wu"].shape[2])
        pairs = (
            (R["slopes"].at[l, :, cols], R["g_hid"].at[:, cols]), (R["actives"].at[l, :, cols], R["active"].at[:, cols]),
            (R["w_down"].at[l, cols], R["wd"].at[cols]), (R["w_up"].at[l, i], R["wu"].at[i]),
        )
        return [pltpu.make_async_copy(src, dst, sem.at[base + 4 * i + n]) for n, (src, dst) in enumerate(pairs)]

    strip_base = {}

    def load_strips(l):
        strip_base[l] = count[0]
        count[0] += 4 * NARROW
        for i in range(NARROW):
            for copy in strip_copies(l, i, strip_base[l]):
                copy.start()

    def strip_waits(l):
        def wait(i):
            for copy in strip_copies(l, i, strip_base[l]):
                copy.wait()

        return wait

    far = [0]

    def remote(src, dst, n, peer):
        return pltpu.make_async_remote_copy(
            src_ref=src, dst_ref=dst, send_sem=R["out_sem"].at[n], recv_sem=R["in_sem"].at[n],
            device_id=peer, device_id_type=MESH,
        )

    def new_far():
        far[0] += 1
        return far[0] - 1

    def columns_start(n, src, b, at):
        start = (c // group) * LEN + place_of(group, g, b) * BLOCK
        to, rows = R["columns"].at[n, pl.ds(pl.multiple_of(start, BLOCK), BLOCK)], pl.ds(b * BLOCK, BLOCK)
        begin("columns%d" % (n * per + b), (src.at[c, rows], to))
        for d in range(1, n_col):
            remote(src.at[col_peer(d), rows], to, at, (r, col_peer(d))).start()

    def columns_end(n, at):
        for b in range(per):
            waits("columns%d" % (n * per + b))
        ref = R["columns"].at[n, pl.ds(0, (n_col - 1) * tokens)]
        remote(ref, ref, at, (r, col_peer(1))).wait()

    ends = {}

    def spread(kind, l):
        src, land, at = R["grads_" + kind], R["land_" + kind].at[l], new_far()
        begin("own_%s%d" % (kind, l), (src.at[c], land.at[c]))
        for d in range(1, n_col):
            remote(src.at[col_peer(d)], land.at[c], at, (r, col_peer(d))).start()
        ends["spread", kind, l] = at

    def spread_sent(kind, l):
        if l < layers:
            ref = R["land_" + kind].at[l, pl.ds(0, n_col - 1)]
            remote(ref, ref, ends["spread", kind, l], (r, col_peer(1))).wait_send()

    def add_load(kind, l):
        land = R["land_" + kind].at[l]
        ref = land.at[pl.ds(0, n_col - 1)]
        remote(ref, ref, ends["spread", kind, l], (r, col_peer(1))).wait_recv()
        waits("own_%s%d" % (kind, l))
        begin("stage_" + kind, (land, R["stage_" + kind]))

    def add(kind, l):
        stage, total = R["stage_" + kind], R["sum_" + kind]
        add_sent(kind, l + 1)
        waits("stage_" + kind)
        for q in range(seqs):
            value = sum(stage[q * group + n].astype(F32) for n in range(group))
            total[q] = value.astype(BF16)
        parts, at = R["parts_" + kind], new_far()
        begin("part_%s%d" % (kind, l), (total, parts.at[l, r]))
        for q in range(1, n_row):
            remote(total, parts.at[l, r], at, row_peer(q)).start()
        ends["add", kind, l] = at

    def added(kind, l):
        ref = R["parts_" + kind].at[l, pl.ds(0, n_row - 1)]
        return remote(ref, ref, ends["add", kind, l], row_peer(1))

    def add_sent(kind, l):
        if l < layers:
            waits("part_%s%d" % (kind, l))
            added(kind, l).wait_send()

    def part_copy(l, j, i, at):
        to = c - g + lax.rem(g - j + group, group)
        strip = pl.ds(i, 1)
        return remote(R["part%d" % j].at[strip], R["in_part"].at[l, j - 1, strip], at[j] + i, (r, to))

    def back_strip(l, i, at):
        kvs = [R["kv"]] + [R["peer"].at[j] for j in range(group - 1)]
        gkvs = [R["part%d" % j] for j in range(group)]
        attend_back_strip(held, bias, g, i, R["gq"], R["lse"], R["att"], R["low"], kvs, R["gq"], gkvs)
        for j in range(1, group):
            part_copy(l, j, i, at).start()

    def load_qkv(l):
        begin("qkv", *[
            (R["w_qkv"].at[l, i], R["wq"].at[i // 2, :, columns(i % 2, 384)]) for i in range(NARROW)
        ])

    def load_mlp(l):
        load_strips(l)
        begin("proj", (R["w_proj"].at[l], R["wp"]))

    def load_attention(l):
        begin("mid", (R["mids"].at[l], R["mid"]))
        begin("att", (R["atts"].at[l], R["att"]))
        begin("q", (R["qs"].at[l], R["gq"]))
        begin("kv", (R["kvs"].at[l], R["kv"]), (R["peers"].at[l], R["peer"]), (R["lses"].at[l], R["lse"]))

    def block_done(b):
        if b < 0:
            spread("qkv", 0)
            return
        if b == per - 1:
            add("qkv", 0)
        columns_start(1, R["part0"].at[:, :, pl.ds(0, 128)], b, at_grad)
        if b == max(per - 2, 0):
            add_load("qkv", 0)

    last = layers - 1
    begin("cotangent", (R["cotangent"], R["low"]))
    begin("tables", *[(R["in_" + name], R[name]) for name in TABLES + ("vec", "reds")])
    load_mlp(last)
    load_attention(last)
    load_qkv(last)
    at_result, at_grad = new_far(), new_far()
    for b in range(per):
        columns_start(0, R["result"], b, at_result)
    at_ids = new_far()
    begin("ids", (R["ids"], R["all_ids"].at[r]))
    for q in range(1, n_row):
        remote(R["ids"], R["all_ids"].at[r], at_ids, row_peer(q)).start()
    waits("cotangent")

    def widen(rows):
        R["grad"][rows, :] = R["low"][rows, :].astype(F32)

    by_rows(tokens, widen)
    waits("tables")
    for l in reversed(range(layers)):
        t = {name: R[name].at[l] for name in TABLES if "qkv" not in name}
        vec = Vectors(R["vec"], l)
        spread_sent("mlp", l + 1)
        mlp_back_stage(
            vec, R["grad"], R["active"], R["g_hid"], R["mid"], R["att"], R["low"], R["total"], R["wp"], R["wu"],
            R["wd"], R["reds"].at[l], {k: (v if k in ("low_down", "up_up") else v[...]) for k, v in t.items()},
            R["grads_mlp"], R["total2"], waits, strip_waits(l),
        )
        spread("mlp", l)
        if l > 0:
            load_mlp(l - 1)
        begin("x", (R["tokens"] if l == 0 else R["xs"].at[l - 1], R["x0"] if l == 0 else R["mid"]))
        waits("q")
        waits("kv")
        at = [far[0] + j * NARROW for j in range(group)]
        far[0] += group * NARROW
        half = NARROW // 2
        if l < last:
            add_load("qkv", l + 1)
        each(half, lambda i: back_strip(l, i, at))
        add_load("mlp", l)
        if l < last:
            add("qkv", l + 1)
        add("mlp", l)
        each(half, lambda i: back_strip(l, half + i, at))
        for i in range(NARROW):
            for j in range(1, group):
                part_copy(l, j, i, at).wait_recv()
            begin(("part", i), *[(R["in_part"].at[l, j, i], R["peer"].at[j, i]) for j in range(group - 1)])
        parts = [R["part0"]] + [R["peer"].at[j] for j in range(group - 1)]
        spread_sent("qkv", l + 1)

        def put(rows, value):
            if l > 0:
                R["grad"][rows, :] = value
            else:
                for i in range(NARROW):
                    R["part0"][i, rows, :128] = value[:, i * 128 : (i + 1) * 128].astype(BF16)

        qkv_back_stage(
            vec, R["x0"] if l == 0 else R["mid"], R["total2"], R["gq"], parts, R["total"], R["g_red"], R["low"],
            R["wq"], R["reds"].at[l, 0], R["low_qkv"].at[l], R["up_qkv"].at[l], R["grads_qkv"], put, waits,
            None if l > 0 else block_done,
        )
        if l > 0:
            spread("qkv", l)
        for i in range(NARROW):
            for j in range(1, group):
                part_copy(l, j, i, at).wait_send()
        if l > 0:
            load_qkv(l - 1)
            load_attention(l - 1)
    columns_end(0, at_result)
    columns_end(1, at_grad)
    waits("ids")
    rest = R["all_ids"].at[pl.ds(0, n_row - 1)]
    remote(rest, rest, at_ids, row_peer(1)).wait()
    for kind in ("mlp", "qkv"):
        spread_sent(kind, 0)
        add_sent(kind, 0)
        for l in range(layers):
            added(kind, l).wait_recv()


def backward(n_row, n_col, group, outs, tables, ids):
    layers, _, dim, _ = outs["qkv"].shape
    hidden = outs["down"].shape[1]
    mine = outs["tokens"].shape[0]
    rank = tables[0].shape[1]
    seqs = n_col // group
    strip = (NARROW, mine)
    near, far = pl.BlockSpec(memory_space=pltpu.VMEM), pl.BlockSpec(memory_space=pltpu.HBM)
    small = list(zip(TABLES, tables)) + [("vec", outs["vec"]), ("reds", outs["reds"])]
    inputs = [("in_" + name, table, far) for name, table in small] + [("ids", ids, far)]
    for name in ("active", "slope", "mid", "att", "q", "kv", "peer", "lse", "x"):
        inputs.append((name + "s", outs["saved_" + name], far))
    inputs += [("w_" + name, outs[name], far) for name in KINDS]
    inputs += [(name, outs[name], far) for name in ("tokens", "cotangent", "result")]
    sizes = {"mlp": 512 + 2 * hidden // NARROW, "qkv": 512}
    outputs = [
        ("columns", (2, n_col * mine, 128), BF16, far),
        ("all_ids", (n_row,) + ids.shape, F32, far),
        ("in_part", (layers, group - 1) + strip + (256,), BF16, far),
    ]
    scratch = [
        ("gq", strip + (128,), BF16), ("kv", strip + (256,), BF16), ("peer", (group - 1,) + strip + (256,), BF16),
        ("lse", (NARROW, 8, mine), F32), ("total", (mine, dim), F32), ("total2", (mine, dim), F32),
        ("grad", (mine, dim), F32), ("mid", (mine, dim), F32), ("low", (mine, dim), BF16), ("att", (mine, dim), BF16),
        ("x0", (mine, dim), BF16), ("active", (mine, hidden), BF16), ("g_hid", (mine, hidden), BF16),
        ("g_red", (mine, rank), BF16), ("wq", (NARROW // 2, dim, 768), BF16), ("wp", (dim, dim), BF16),
        ("wu", (NARROW, dim, hidden // NARROW), BF16), ("wd", (hidden, dim), BF16),
    ]
    scratch += [("part%d" % j, strip + (256,), BF16) for j in range(group)]
    scratch += [(name, table.shape, table.dtype) for name, table in small]
    for kind, size in sizes.items():
        outputs.append(("land_" + kind, (layers, n_col, rank, size), BF16, far))
        outputs.append(("parts_" + kind, (layers, n_row, seqs, rank, size), BF16, far))
        scratch.append(("grads_" + kind, (NARROW, rank, size), BF16))
        scratch.append(("stage_" + kind, (n_col, rank, size), BF16))
        scratch.append(("sum_" + kind, (seqs, rank, size), BF16))
    scratch = [(name, pltpu.VMEM(shape, kind)) for name, shape, kind in scratch]
    scratch += [
        ("sem", pltpu.SemaphoreType.DMA((72 * layers + 16,))),
        ("out_sem", pltpu.SemaphoreType.DMA(((4 + group * NARROW) * layers + 4,))),
        ("in_sem", pltpu.SemaphoreType.DMA(((4 + group * NARROW) * layers + 4,))),
    ]
    names = [x[0] for x in inputs] + [x[0] for x in outputs] + [x[0] for x in scratch]
    made = pl.pallas_call(
        functools.partial(backward_body, layers, group, n_row, n_col, tuple(names)),
        out_shape=[shape_of(shape, kind) for _, shape, kind, _ in outputs],
        in_specs=[spec for _, _, spec in inputs],
        out_specs=[spec for _, _, _, spec in outputs],
        scratch_shapes=[shape for _, shape in scratch],
        compiler_params=pltpu.CompilerParams(
            collective_id=1, has_side_effects=True, vmem_limit_bytes=62 * 2**20
        ),
        name="backward",
    )(*[array for _, array, _ in inputs])
    return dict(zip([x[0] for x in outputs], made))


def place_body(layers, names, *refs):
    R = dict(zip(names, refs))
    sem, ends = R["sem"], []

    def copy(src, dst, n):
        made = pltpu.make_async_copy(src, dst, sem.at[n])
        made.start()
        return made

    loads = [copy(R["columns"].at[n], R["low"].at[n], n) for n in range(2)]
    ins = {kind: copy(R["parts_" + kind], R["in_" + kind], 2 + n) for n, kind in enumerate(SITES)}
    for n in range(2):
        loads[n].wait()
        R["wide"][n] = R["low"][n].astype(F32)
        ends.append(copy(R["wide"].at[n], R["column_out%d" % n], 4 + n))
    rows, adapters, rank = R["ids"].shape[0], R["keep0"].shape[1], R["keep0"].shape[2]
    sequences = R["in_qkv"].shape[1]
    shape = (adapters * rank, sequences * rank)
    down, across = [lax.broadcasted_iota(jnp.int32, shape, axis) for axis in (0, 1)]
    weights = {}
    for site in range(4):
        chosen = jnp.zeros((1, shape[1]), F32)
        for q in range(sequences):
            value = R["ids"][q // (sequences // rows), q % (sequences // rows), site]
            chosen = jnp.where(across[:1] // rank == q, value, chosen)
        same = (chosen == (down // rank).astype(F32)) & (down % rank == across % rank)
        weights[site] = jnp.where(same, 1.0, 0.0).astype(BF16)
    number = 0
    for kind in ("qkv", "mlp"):
        ins[kind].wait()
        stage = R["in_" + kind]
        sequences, rank = stage.shape[1:3]
        at = 0
        for site, size in zip(SITES[kind], R["sizes"][kind]):
            out, keep = R["out%d" % number], R["keep%d" % number]
            for l in range(layers):
                part = stage[l, :, :, at : at + size]
                made = dot(weights[site], part.reshape(sequences * rank, size)).reshape(-1, rank, size)
                if number == 1:
                    for n in range(3):
                        keep[l, :, n] = made[:, :, n * 128 : (n + 1) * 128]
                else:
                    keep[l] = made
            ends.append(copy(keep, out, 6 + number))
            at += size
            number += 1
    for end in ends:
        end.wait()


def place(made, sizes, adapters):
    layers, rank = made["parts_qkv"].shape[0], made["parts_qkv"].shape[-2]
    hbm = pl.BlockSpec(memory_space=pltpu.HBM)
    columns = made["columns"]
    parts = {kind: made["parts_" + kind].reshape(layers, -1, rank, sum(sizes[kind])) for kind in SITES}
    widths = [size for kind in ("qkv", "mlp") for size in sizes[kind]]
    inputs = [("ids", made["all_ids"], pl.BlockSpec(memory_space=pltpu.SMEM)), ("columns", columns, hbm)]
    inputs += [("parts_" + kind, parts[kind], hbm) for kind in SITES]
    outputs = [("column_out%d" % n, columns.shape[1:], F32) for n in range(2)]
    shapes = [(layers, adapters, rank, size) for size in widths]
    shapes[1] = (layers, adapters, 3, rank, 128)
    outputs += [("out%d" % n, shape, F32) for n, shape in enumerate(shapes)]
    scratch = [("low", pltpu.VMEM(columns.shape, BF16)), ("wide", pltpu.VMEM(columns.shape, F32))]
    scratch += [("in_" + kind, pltpu.VMEM(parts[kind].shape, BF16)) for kind in SITES]
    scratch += [("keep%d" % n, pltpu.VMEM(shape, F32)) for n, shape in enumerate(shapes)]
    scratch.append(("sem", pltpu.SemaphoreType.DMA((6 + len(widths),))))
    names = [x[0] for x in inputs] + [x[0] for x in outputs] + [x[0] for x in scratch]

    def body(*refs):
        place_body(layers, names + ["sizes"], *refs, sizes)

    return pl.pallas_call(
        body,
        out_shape=[shape_of(shape, kind) for _, shape, kind in outputs],
        in_specs=[spec for _, _, spec in inputs],
        out_specs=[hbm] * len(outputs),
        scratch_shapes=[shape for _, shape in scratch],
        compiler_params=PARAMS,
        name="place",
    )(*[array for _, array, _ in inputs])


def to_rows_body(held, x, out):
    n = 0
    for s in range(x.shape[0] // (len(held) * len(held[0]))):
        for g in range(len(held)):
            for place in held[g]:
                start = (s * BLOCKS + place) * BLOCK
                out[start : start + BLOCK, :] = x[n].astype(F32)
                n += 1


def to_rows(held, x):
    blocks, _, width = x.shape
    return pl.pallas_call(
        functools.partial(to_rows_body, held),
        out_shape=shape_of((blocks * BLOCK, width), F32),
        compiler_params=PARAMS,
        name="to_rows",
    )(x)


def pick_body(width, units, ids, *refs):
    tables, raise_qkv, vectors, every = refs[:7], refs[7], refs[8:16], refs[16]
    qkv_b, up_b, proj_b, down_b, gain1, shift1, gain2, shift2 = vectors
    outs, raise_out, vector, ids_rows = refs[17:24], refs[24], refs[25], refs[26]
    for ref, out in zip(tables, outs):
        out[...] = ref[...]
    layers = raise_qkv.shape[0]
    vector[...] = jnp.zeros_like(vector)
    for l in range(layers):
        for n in range(3):
            row = raise_qkv[l, n]
            for i in range(NARROW):
                raise_out[l, i, :, n * 128 : (n + 1) * 128] = row[:, i * 128 : (i + 1) * 128]
            vector[4 * l : 4 * l + 1, n * width : (n + 1) * width] = qkv_b[n, l : l + 1, :].astype(F32)
        vector[4 * l + 1 : 4 * l + 2, :units] = up_b[l : l + 1, :].astype(F32)
        for n, ref in enumerate((proj_b, down_b, gain1, shift1, gain2, shift2)):
            row, lane = 4 * l + 2 + n // 4, n % 4 * width
            vector[row : row + 1, lane : lane + width] = ref[l : l + 1, :].astype(F32)
    ids_rows[...] = jnp.zeros_like(ids_rows)
    ids_rows[: every.shape[0], : every.shape[1]] = every[...].astype(F32)


def pick(group, adapter_ids, tables, raise_qkv, vectors):
    layers, _, _, rank, dim = raise_qkv.shape
    width, units = vectors[2].shape[1], vectors[1].shape[1]

    def chosen(site, shape):
        rest = (0,) * (len(shape) - 2)
        return pl.BlockSpec(
            (shape[0], None) + shape[2:], lambda i, ids: (0, ids[lax.axis_index("col") // group, site]) + rest
        )

    def whole(shape):
        return pl.BlockSpec(shape, lambda i, ids: (0,) * len(shape))

    shapes = [(table.shape[:1] + table.shape[2:], BF16) for _, table in tables]
    shapes += [((layers, NARROW, rank, 384), BF16), ((4 * layers, 512), F32), ((8, 128), F32)]
    return pl.pallas_call(
        functools.partial(pick_body, width, units),
        grid_spec=pltpu.PrefetchScalarGridSpec(
            num_scalar_prefetch=1,
            grid=(1,),
            in_specs=[chosen(site, table.shape) for site, table in tables]
            + [chosen(0, raise_qkv.shape)]
            + [whole(x.shape) for x in vectors]
            + [whole(adapter_ids.shape)],
            out_specs=[whole(shape) for shape, _ in shapes],
        ),
        out_shape=[shape_of(shape, kind) for shape, kind in shapes],
        compiler_params=PARAMS,
        name="pick",
    )(adapter_ids, *[table for _, table in tables], raise_qkv, *vectors, adapter_ids)


def shards(mesh_shape, *args):
    (
        tokens, cotangent, adapter_ids, qkv_weight, qkv_bias, proj_weight, proj_bias,
        up_weight, up_bias, down_weight, down_bias, first_gain, first_shift, second_gain,
        second_shift, qkv_lower, qkv_raise, proj_lower, proj_raise, up_lower, up_raise,
        down_lower, down_raise,
    ) = args
    n_row, n_col = mesh_shape
    layers, adapters, dim, rank = qkv_lower.shape
    rows, width = tokens.shape
    units = up_weight.shape[2]
    seqs = rows // LEN
    group = n_col // seqs
    held = positions(group)
    per = BLOCKS // group
    mine = per * BLOCK
    merge = 128 // width
    c = lax.axis_index("col")
    g = lax.rem(c, group)
    def turned(table):
        return jnp.swapaxes(table, 2, 3)

    *picked, vector, ids_rows = pick(
        group, adapter_ids,
        [
            (0, turned(qkv_lower)), (1, turned(proj_lower)), (1, proj_raise), (2, turned(up_lower)), (2, up_raise),
            (3, turned(down_lower)), (3, down_raise),
        ],
        qkv_raise.transpose(0, 1, 3, 2, 4),
        (qkv_bias.transpose(1, 0, 2), up_bias, proj_bias, down_bias, first_gain, first_shift, second_gain, second_shift),
    )
    tables = [picked[0], picked[7]] + list(picked[1:7])
    fused = FUSED and width == 128
    if width == 128:
        qkv_shard = qkv_weight.transpose(0, 2, 1, 3)
    else:
        qkv_shard = qkv_weight.reshape(layers, -1, 3 * width)
    outs = gather_inputs(
        n_row, n_col, group, qkv_shard, proj_weight, up_weight,
        down_weight, tokens, cotangent, vector, tables if fused else None
    )
    g_one = g.reshape(1)

    def peer_values(x, step):
        pairs = [(q, q - q % group + (q + step) % group) for q in range(n_col)]
        return lax.ppermute(x, "col", pairs)

    def to_columns(x):
        if merge > 1:
            x = x.reshape(NARROW, mine, merge, width).transpose(0, 2, 1, 3).reshape(n_col, mine, width)
        x = lax.all_to_all(x, "col", split_axis=0, concat_axis=0, tiled=True)
        return to_rows(held, x.reshape(n_col * per, BLOCK, width))

    if not fused:
        x = outs["tokens"].astype(F32)
        kept = {name: [] for name in SAVED + ("reds",)}
        for l in range(layers):
            q, kv, red = qkv_kernel(l, x, outs["vec"], outs["qkv"], tables[0], tables[1])
            kvs = [kv] + [peer_values(kv, s) for s in range(1, group)]
            att, lse = attend_kernel(group, g_one, q, kvs)
            mid, x, active, slope, reds = mlp_kernel(
                l, l == layers - 1, x, att, outs["vec"], outs["proj"], outs["up"], outs["down"], tables[2:]
            )
            reds = jnp.concatenate([red[None], reds])
            peer = jnp.stack(kvs[1:]) if group > 1 else kv[None][:0]
            for name, value in zip(SAVED + ("reds",), (q, kv, peer, att, lse, mid, active, slope, x, reds)):
                kept[name].append(value)
        for name in SAVED:
            outs["saved_" + name] = jnp.stack(kept[name][: layers - 1] if name == "x" else kept[name])
        outs["reds"] = jnp.stack(kept["reds"])
        outs["result"] = x
    if fused:
        made = backward(n_row, n_col, group, outs, tables, ids_rows)
        sizes = {"qkv": (128, 384), "mlp": (128, 128, 128, units, units, 128)}
        sums = place(made, sizes, adapters)
        final = list(sums[:2])
        for number, p in enumerate(sums[2:]):
            if number == 1:
                p = p.transpose(0, 1, 3, 2, 4)
            elif number % 2 == 0:
                p = p.transpose(0, 1, 3, 2)
            final.append(p)
        return tuple(final)

    result = to_columns(outs["result"])

    onehot = (adapter_ids.T[:, :, None] == jnp.arange(adapters)[None, None, :]).astype(BF16)

    def all_rows(x):
        pairs = [[(q, (q + s) % n_row) for q in range(n_row)] for s in range(1, n_row)]
        return [x] + [lax.ppermute(x, "row", pair) for pair in pairs]

    onehots = jnp.concatenate(all_rows(onehot), axis=1)

    def collect(parts, named):
        if merge > 1:
            pieces, at = [], 0
            for _, size in named:
                piece = parts[:, :, at : at + size]
                at += size
                if size == 384:
                    piece = piece.reshape(NARROW, rank, 3, merge, width).transpose(0, 3, 1, 2, 4)
                else:
                    piece = piece.reshape(NARROW, rank, merge, size // merge).transpose(0, 2, 1, 3)
                pieces.append(piece.reshape(n_col, rank, size // merge))
            parts = jnp.concatenate(pieces, axis=2)
        parts = lax.all_to_all(parts, "col", split_axis=0, concat_axis=0, tiled=True)
        parts = parts.reshape((seqs, group) + parts.shape[1:]).astype(F32).sum(axis=1).astype(BF16)
        parts = jnp.concatenate(all_rows(parts), axis=0)
        sums, at = [], 0
        for site, size in named:
            piece = parts[:, :, at : at + size // merge]
            at += size // merge
            sums.append(jnp.einsum("sa,srn->arn", onehots[site], piece, preferred_element_type=F32))
        return sums

    wide = outs["down"].shape[1] // NARROW
    grads, carried = [None] * layers, None
    for l in reversed(range(layers + 1)):
        lq, lm = (l if l < layers else None), (l - 1 if l > 0 else None)
        made = back_kernel(lq, lm, group, g_one, outs, tables, carried)
        if lm is not None:
            grads[lm] = collect(made["grads_mlp"], [(1, 128), (1, 128), (2, 128), (2, wide), (3, wide), (3, 128)])
            parts = [made["out_part%d" % s] for s in range(group)]
            parts = [parts[0]] + [peer_values(parts[s], group - s) for s in range(1, group)]
            carried = (made["out_g_mid"], made["out_gq"], parts)
        if lq is not None:
            grads[lq] = collect(made["grads_qkv"], [(0, 128), (0, 384)]) + grads[lq]
    grad = made["out"]
    input_grad = to_columns(grad)

    final = []
    for number in range(8):
        p = jnp.stack([grads[l][number] for l in range(layers)])
        if number == 1:
            p = p.reshape(layers, adapters, rank, 3, width)
        elif number % 2 == 0:
            p = p.transpose(0, 1, 3, 2)
        final.append(p)
    return (result, input_grad) + tuple(final)


def solution(mesh):
    mesh_shape = (mesh.shape["row"], mesh.shape["col"])
    return jax.shard_map(
        functools.partial(shards, mesh_shape),
        mesh=mesh,
        in_specs=(
            P("row", "col"), P("row", "col"), P("row", None),
            P(None, "row", None, "col"), P(None, None, "col"),
            P(None, "col", "row"), P(None, "col"),
            P(None, "row", "col"), P(None, "col"),
            P(None, "col", "row"), P(None, "col"),
            P(None, "col"), P(None, "col"), P(None, "col"), P(None, "col"),
            P(), P(), P(), P(), P(), P(), P(), P(),
        ),
        out_specs=(
            P("row", "col"), P("row", "col"),
            P(None, None, "col", None), P(None, None, None, None, "col"),
            P(None, None, "col", None), P(None, None, None, "col"),
            P(None, None, "col", None), P(None, None, None, "col"),
            P(None, None, "col", None), P(None, None, None, "col"),
        ),
        check_vma=False,
    )
```

profile of v0, /device:TPU:0, one launch (start us, length us, event | category | flops | bytes accessed | tf_op | source)
XLA Modules:
  0.0 350.9 jit_solution(13196012161497811575)
XLA Ops:
  0.7 3.0 pick.1
  3.6 229.4 %gather_inputs.1 = (bf16[2,8,4,2,128,384]{5,4,3,2,1,0:T(8,128)(2,1)}, bf16[2,8,2,64,1024]{4,3,2,1,0:T(8,128)(2,1)}, bf16[2,8,4,4,64,512]{5,4,3,2,1,0:T(8,128)(2,...) custom-call(bf16[2,3,256,128]{3,2,1,0:T(8,128)(2,1)} %bitcast.29, ...), custom_call_target="tpu_custom_call" | custom-call | tf_op jit(solution)/shard_map/gather_inputs/pallas_call | solution.py:901
  233.1 112.6 %backward.1 = (bf16[2,4096,128]{2,1,0:T(8,128)(2,1)}, f32[4,8,128]{2,1,0:T(8,128)}, bf16[2,1,8,512,256]{4,3,2,1,0:T(8,128)(2,1)}, bf16[2,8,16,1536]{3,2,1,0:T(8,...) custom-call(bf16[2,16,1024]{2,1,0:T(8,128)(2,1)} %get-tuple-element., ...), custom_call_target="tpu_custom_call" | custom-call | tf_op jit(solution)/shard_map/backward/pallas_call | solution.py:1625
  345.7 5.0 %place.1 = (f32[4096,128]{1,0:T(8,128)}, f32[4096,128]{1,0:T(8,128)}, f32[2,8,16,128]{3,2,1,0:T(8,128)}, f32[2,8,3,16,128]{4,3,2,1,0:T(8,128)}, f32[2,8,16,128]{...) custom-call(f32[4,8,128]{2,1,0:T(8,128)} %get-tuple-element.80.refs_, ...), custom_call_target="tpu_custom_call" | custom-call | tf_op jit(solution)/shard_map/place/pallas_call | solution.py:1710
where the time goes:
time: 357 us; the launch traced here: 351 us
  Pallas kernels  350 us (98%)
    pallas_call x1, Pallas kernels, gather_inputs(): pl.pallas_call(functools.partial(gather_body, n_row, n_col, layers, group...  229 us
    pallas_call x1, Pallas kernels, backward(): pl.pallas_call(functools.partial(backward_body, layers, group, n_row, n_c...  113 us

commit v1 on v0

--- a/solution.py
+++ b/solution.py
@@ -23,7 +23,7 @@
 ROW_FIRST = (("z", 0, 1), ("z", 1, 0))
 ROW_SECOND = ((0, "z", 1), (1, "z", 0))
 ORDERS = (
-    {"qkv": (ROW_FIRST,), "proj": (ROW_SECOND,), "up": (ROW_FIRST,) * 2, "down": (ROW_SECOND, ROW_FIRST)},
+    {"qkv": (ROW_FIRST,), "proj": (ROW_SECOND,), "up": (ROW_FIRST,) * 2, "down": (ROW_FIRST, ROW_SECOND)},
     {"qkv": (ROW_SECOND,), "proj": (ROW_FIRST,), "up": (ROW_SECOND,) * 2, "down": (ROW_SECOND,) * 2},
 )
 CUTS = {kind: 2 * len(pairs) for kind, pairs in ORDERS[0].items()}
@@ -1540,10 +1540,19 @@
             add("qkv", l + 1)
         add("mlp", l)
         each(half, lambda i: back_strip(l, half + i, at))
-        for i in range(NARROW):
-            for j in range(1, group):
-                part_copy(l, j, i, at).wait_recv()
-            begin(("part", i), *[(R["in_part"].at[l, j, i], R["peer"].at[j, i]) for j in range(group - 1)])
+
+        def fetch_parts(first, end):
+            for i in range(first, end):
+                for j in range(1, group):
+                    part_copy(l, j, i, at).wait_recv()
+                begin(("part", i), *[(R["in_part"].at[l, j, i], R["peer"].at[j, i]) for j in range(group - 1)])
+
+        def part_waits(name):
+            if name == ("part", 2):
+                fetch_parts(NARROW - 3, NARROW)
+            waits(name)
+
+        fetch_parts(0, NARROW - 3)
         parts = [R["part0"]] + [R["peer"].at[j] for j in range(group - 1)]
         spread_sent("qkv", l + 1)
 
@@ -1556,7 +1565,7 @@
 
         qkv_back_stage(
             vec, R["x0"] if l == 0 else R["mid"], R["total2"], R["gq"], parts, R["total"], R["g_red"], R["low"],
-            R["wq"], R["reds"].at[l, 0], R["low_qkv"].at[l], R["up_qkv"].at[l], R["grads_qkv"], put, waits,
+            R["wq"], R["reds"].at[l, 0], R["low_qkv"].at[l], R["up_qkv"].at[l], R["grads_qkv"], put, part_waits,
             None if l > 0 else block_done,
         )
         if l > 0:

time: 357 us -> 356 us (level)
  no operation moved by 1% of the time
where the time goes in v1:
time: 356 us; the launch traced here: 351 us
  Pallas kernels  350 us (98%)
    pallas_call x1, Pallas kernels, gather_inputs(): pl.pallas_call(functools.partial(gather_body, n_row, n_col, layers, group...  230 us
    pallas_call x1, Pallas kernels, backward(): pl.pallas_call(functools.partial(backward_body, layers, group, n_row, n_c...  112 us

profile of v1, /device:TPU:0, one launch (start us, length us, event | category | flops | bytes accessed | tf_op | source)
XLA Modules:
  0.0 350.5 jit_solution(16378288367731624437)
XLA Ops:
  0.7 3.0 pick.1
  3.6 230.0 %gather_inputs.1 = (bf16[2,8,4,2,128,384]{5,4,3,2,1,0:T(8,128)(2,1)}, bf16[2,8,2,64,1024]{4,3,2,1,0:T(8,128)(2,1)}, bf16[2,8,4,4,64,512]{5,4,3,2,1,0:T(8,128)(2,...) custom-call(bf16[2,3,256,128]{3,2,1,0:T(8,128)(2,1)} %bitcast.29, ...), custom_call_target="tpu_custom_call" | custom-call | tf_op jit(solution)/shard_map/gather_inputs/pallas_call | solution.py:901
  233.7 111.6 %backward.1 = (bf16[2,4096,128]{2,1,0:T(8,128)(2,1)}, f32[4,8,128]{2,1,0:T(8,128)}, bf16[2,1,8,512,256]{4,3,2,1,0:T(8,128)(2,1)}, bf16[2,8,16,1536]{3,2,1,0:T(8,...) custom-call(bf16[2,16,1024]{2,1,0:T(8,128)(2,1)} %get-tuple-element., ...), custom_call_target="tpu_custom_call" | custom-call | tf_op jit(solution)/shard_map/backward/pallas_call | solution.py:1634
  345.3 5.0 %place.1 = (f32[4096,128]{1,0:T(8,128)}, f32[4096,128]{1,0:T(8,128)}, f32[2,8,16,128]{3,2,1,0:T(8,128)}, f32[2,8,3,16,128]{4,3,2,1,0:T(8,128)}, f32[2,8,16,128]{...) custom-call(f32[4,8,128]{2,1,0:T(8,128)} %get-tuple-element.80.refs_, ...), custom_call_target="tpu_custom_call" | custom-call | tf_op jit(solution)/shard_map/place/pallas_call | solution.py:1719
